TPU v7x, 32 devices: a whole 2x2x4 slice. The times are simulated.
32 devices in a mesh: seq: 16 (over z, x, core), tp: 2 (over y).
Axes of the slice: x: 2, y: 2, z: 4, core: 2. Of those that a mesh axis runs over, the one named last changes fastest.
Arguments:
- queries: float32 [4096, 4096], P(('seq', 'tp')), may hold values from -8 to 8
- keys: float32 [4096, 2048], P(('seq', 'tp')), may hold values from -8 to 8
- values: float32 [4096, 2048], P(('seq', 'tp')), may hold values from -6 to 6
- out_grad: float32 [4096, 4096], P(('seq', 'tp')), may hold values from -6 to 6
- positions: int32 [4096], P('seq'), may hold values from 0 to 2047, as said below
Outputs:
- attended: float32 [4096, 4096], P(('seq', 'tp'))
- grad_queries: float32 [4096, 4096], P(('seq', 'tp'))
- grad_keys: float32 [4096, 2048], P(('seq', 'tp'))
- grad_values: float32 [4096, 2048], P(('seq', 'tp'))
Inputs may be any that keep to these rules, and one draw needn't show every extreme that they name: `positions`: each token's position within its document: one more than the token before, except at a document's first token, where it is 0; the slice's first document may have begun before the slice.
All inputs are finite; a program needn't handle non-finite values.
Results may differ from a plain program's by a relative error of at most 0.0005.
Values sent between devices are 32-bit elements; how exact they have to be, the bound alone decides.
A program may use at most 128 MiB of HBM per device.

v0:
```python
import functools

import jax
import jax.numpy as jnp
from jax import lax
from jax.experimental import pallas as pl
from jax.experimental.pallas import tpu as pltpu
from jax.sharding import PartitionSpec as P

HEAD_DIM = 128
WINDOW = 1024
CHUNKS = 2

score_scale = 168.0 ** (-0.5)
neg_fill = -1e30
f32 = jnp.float32
bf16 = jnp.bfloat16


def split(x):
    hi = x.astype(bf16)
    lo = (x - hi.astype(f32)).astype(bf16)
    return hi, lo


def mm(a, b, dims):
    return lax.dot_general(a, b, (dims, ((), ())), preferred_element_type=f32)


NT = ((1,), (1,))
NN = ((1,), (0,))
TN = ((0,), (0,))


def attend(reach1, group, low_ref, pos_ref, kidx_ref, q_ref, g_ref, *refs):
    k_refs = refs[:reach1]
    v_refs = refs[reach1 : 2 * reach1]
    o_ref, dq_ref = refs[2 * reach1 : 2 * reach1 + 2]
    dk_refs = refs[2 * reach1 + 2 : 3 * reach1 + 2]
    dv_refs = refs[3 * reach1 + 2 : 4 * reach1 + 2]
    s_ref, ph_ref, pl_ref = refs[4 * reach1 + 2 :]
    d = HEAD_DIM
    tok = q_ref.shape[0]

    def stacked(ref):
        return jnp.concatenate([ref[:, r * d : (r + 1) * d] for r in range(group)], axis=0)

    low = jnp.concatenate([low_ref[...]] * group, axis=0)
    pos = jnp.concatenate([pos_ref[...]] * group, axis=0)
    q = stacked(q_ref) * score_scale
    qh, ql = split(q)
    qhl = jnp.concatenate([qh, ql], axis=1)
    top = None
    for j in range(reach1):
        kh, kl = split(k_refs[j][...])
        s = mm(qhl, jnp.concatenate([kh, kh], axis=1), NT) + mm(qh, kl, NT)
        kid = kidx_ref[j : j + 1, :]
        s = jnp.where((kid >= low) & (kid <= pos), s, neg_fill)
        s_ref[j] = s
        m = jnp.max(s, axis=1, keepdims=True)
        top = m if top is None else jnp.maximum(top, m)
    total = jnp.zeros_like(top)
    acc = jnp.zeros((group * tok, d), f32)
    for j in range(reach1):
        p = jnp.exp(s_ref[j] - top)
        total = total + jnp.sum(p, axis=1, keepdims=True)
        ph, plo = split(p)
        ph_ref[j] = ph
        pl_ref[j] = plo
        vh, vl = split(v_refs[j][...])
        both = mm(ph, jnp.concatenate([vh, vl], axis=1), NN)
        acc = acc + (both[:, :d] + both[:, d:]) + mm(plo, vh, NN)
    inv = 1.0 / total
    out = acc * inv
    for r in range(group):
        o_ref[:, r * d : (r + 1) * d] = out[r * tok : (r + 1) * tok]
    grad = stacked(g_ref) * inv
    delta = jnp.sum(grad * out, axis=1, keepdims=True)
    gh, gl = split(grad)
    ghl = jnp.concatenate([gh, gl], axis=1)
    dq = jnp.zeros((group * tok, d), f32)
    for j in range(reach1):
        vh, vl = split(v_refs[j][...])
        kh, kl = split(k_refs[j][...])
        ph, plo = ph_ref[j], pl_ref[j]
        dp = mm(ghl, jnp.concatenate([vh, vh], axis=1), NT) + mm(gh, vl, NT)
        ds = (ph.astype(f32) + plo.astype(f32)) * (dp - delta)
        both = mm(ph, ghl, TN)
        dv_refs[j][...] = both[:, :d] + both[:, d:] + mm(plo, gh, TN)
        sh, sl = split(ds)
        both = mm(sh, qhl, TN)
        dk_refs[j][...] = both[:, :d] + both[:, d:] + mm(sl, qh, TN)
        both = mm(sh, jnp.concatenate([kh, kl], axis=1), NN)
        dq = dq + (both[:, :d] + both[:, d:]) + mm(sl, kh, NN)
    dq = dq * score_scale
    for r in range(group):
        dq_ref[:, r * d : (r + 1) * d] = dq[r * tok : (r + 1) * tok]


def run_attend(low, pos, kidx, q, grad, kv_pieces):
    tok = q.shape[0]
    reach1 = len(kv_pieces)
    kv_cols = kv_pieces[0].shape[1] // 2
    heads = kv_cols // HEAD_DIM
    group = q.shape[1] // kv_cols
    d = HEAD_DIM
    whole = lambda *shape: pl.BlockSpec(shape, lambda h: (0,) * len(shape))
    qspec = pl.BlockSpec((tok, group * d), lambda h: (0, h))
    kspec = pl.BlockSpec((tok, d), lambda h: (0, h))
    vspec = pl.BlockSpec((tok, d), lambda h: (0, h + heads))
    flops = 2 * 6 * 3 * tok * group * tok * reach1 * d * heads
    outs = pl.pallas_call(
        functools.partial(attend, reach1, group),
        grid=(heads,),
        in_specs=[whole(tok, 1), whole(tok, 1), whole(*kidx.shape), qspec, qspec]
        + [kspec] * reach1
        + [vspec] * reach1,
        out_specs=[qspec, qspec] + [kspec] * (2 * reach1),
        out_shape=[jax.ShapeDtypeStruct(q.shape, f32)] * 2
        + [jax.ShapeDtypeStruct((tok, kv_cols), f32)] * (2 * reach1),
        scratch_shapes=[
            pltpu.VMEM((reach1, group * tok, tok), f32),
            pltpu.VMEM((reach1, group * tok, tok), bf16),
            pltpu.VMEM((reach1, group * tok, tok), bf16),
        ],
        compiler_params=pltpu.CompilerParams(vmem_limit_bytes=40 * 2**20),
        cost_estimate=pl.CostEstimate(
            flops=2 * flops, bytes_accessed=4 * (4 * q.size + 20 * tok * kv_cols), transcendentals=0
        ),
    )(low, pos, kidx, q, grad, *kv_pieces, *kv_pieces)
    return outs[0], outs[1], outs[2 : 2 + reach1], outs[2 + reach1 :]


def per_device(queries, keys, values, out_grad, positions):
    seq_size, tp_size = lax.axis_size("seq"), lax.axis_size("tp")
    s = lax.axis_index("seq")
    t = lax.axis_index("tp")
    rows = queries.shape[0]
    tok = rows * tp_size
    pair = tp_size == 2
    kv_local = keys.shape[1] // tp_size
    q_local = queries.shape[1] // tp_size
    chunks = CHUNKS if pair else 1
    kw, qw = kv_local // chunks, q_local // chunks

    def shift_seq(x, route):
        return lax.ppermute(x, "seq", [(a, b) for a, b in route if 0 <= b < seq_size])

    up = [(i, i + 4) for i in range(seq_size)]
    down = [(i, i - 4) for i in range(seq_size)]
    cross = [(i, i ^ 2) for i in range(seq_size)]
    core = [(i, i ^ 1) for i in range(seq_size)]
    swap = [(0, 1), (1, 0)]

    local = jnp.arange(tok, dtype=jnp.int32)
    if pair:
        local = lax.rem(local + t * rows, tok)
        mine, other = positions[:rows], positions[rows:]
        positions = jnp.where(t == 0, positions, jnp.concatenate([other, mine]))
    first = s * tok
    pos = first + local
    low = jnp.maximum(jnp.maximum(pos - positions, pos - (WINDOW - 1)), 0)

    b = s % 4
    base = s - b
    x1, c1 = b // 2 == 1, b % 2 == 1
    p2_block = jnp.where(x1, s - 2, s - 2)
    c_p2 = (s ^ 1) - 2
    c_first = jnp.where(c1, s - 1, s - 3)
    blocks = jnp.stack([s, s - 4, p2_block, c_first, c_p2])
    kidx = blocks[:, None] * tok + local[None, :]

    pos, low = pos[:, None], low[:, None]

    results = []
    for c in range(chunks):
        if pair:
            def part(x, width, who):
                return lax.dynamic_slice_in_dim(x, who * width * chunks + c * width, width, 1)

            def pack(who):
                return jnp.concatenate(
                    [part(queries, qw, who), part(out_grad, qw, who), part(keys, kw, who), part(values, kw, who)],
                    axis=1,
                )

            packed = jnp.concatenate([pack(t), lax.ppermute(pack(1 - t), "tp", swap)], axis=0)
            q, grad, own = packed[:, :qw], packed[:, qw : 2 * qw], packed[:, 2 * qw :]
        else:
            a2a = lambda x: lax.all_to_all(x, "tp", split_axis=1, concat_axis=0, tiled=True)
            q, grad = a2a(queries), a2a(out_grad)
            own = jnp.concatenate([a2a(keys), a2a(values)], axis=1)
        prior = shift_seq(own, up)
        crossed = shift_seq(jnp.where(x1, prior, own), cross)
        near = shift_seq(jnp.where(c1, prior, own), core)
        near_crossed = shift_seq(crossed, core)
        pieces = [own, prior, crossed, near, near_crossed]
        out, dq, dks, dvs = run_attend(low, pos, kidx, q, grad, pieces)
        g_own, g_prior, g_crossed, g_near, g_nc = [
            jnp.concatenate([dk, dv], axis=1) for dk, dv in zip(dks, dvs)
        ]
        near_back = shift_seq(g_near, core)
        g_crossed = g_crossed + shift_seq(g_nc, core)
        zero = jnp.zeros_like(g_own)
        g_own = g_own + jnp.where(c1, zero, near_back)
        g_prior = g_prior + jnp.where(c1, near_back, zero)
        cross_back = shift_seq(g_crossed, cross)
        g_own = g_own + jnp.where(x1, zero, cross_back)
        g_prior = g_prior + jnp.where(x1, cross_back, zero)
        g_own = g_own + shift_seq(g_prior, down)
        if pair:
            full = jnp.concatenate([out, dq, g_own], axis=1)
            results.append((full[:rows], lax.ppermute(full[rows:], "tp", swap)))
        else:
            b2a = lambda x: lax.all_to_all(x, "tp", split_axis=0, concat_axis=1, tiled=True)
            return (b2a(out), b2a(dq), b2a(g_own[:, :kw]), b2a(g_own[:, kw:]))

    def gather(begin, width):
        mine = jnp.concatenate([r[0][:, begin : begin + width] for r in results], axis=1)
        theirs = jnp.concatenate([r[1][:, begin : begin + width] for r in results], axis=1)
        return jnp.where(
            t == 0,
            jnp.concatenate([mine, theirs], axis=1),
            jnp.concatenate([theirs, mine], axis=1),
        )

    return (
        gather(0, qw),
        gather(qw, qw),
        gather(2 * qw, kw),
        gather(2 * qw + kw, kw),
    )


def solution(mesh):
    spec = P(("seq", "tp"), None)
    return jax.shard_map(
        per_device,
        mesh=mesh,
        in_specs=(spec, spec, spec, spec, P("seq")),
        out_specs=(spec, spec, spec, spec),
        check_vma=False,
    )
```

profile of v0, /device:TPU:0, one launch (start us, length us, event | category | flops | bytes accessed | tf_op | source)
XLA Modules:
  0.0 316.8 jit_solution(1261074770187830075)
XLA Ops:
  0.7 2.2 constant_dynamic-slice_fusion.13
  2.8 2.1 constant_dynamic-slice_fusion.12
  7.8 3.0 collective-permute-start.5
  12.1 34.0 %collective-permute-done.5 = f32[128,3072]{1,0:T(8,128)S(1)} collective-permute-done((f32[128,3072]{1,0:T(8,128)S(1)}, f32[128,3072]{1,0:T(8,128)S(1)}, u32[]{:S(2)}, u32[]{:S(2)}) %collective-permute-start.5) | collective-permute-done | bytes 1572896 | tf_op jit(solution)/shard_map/ppermute | solution.py:187
  46.4 1.7 copy-done.5
  48.2 4.2 %collective-permute-start.6 = (f32[256,1024]{1,0:T(8,128)S(1)}, f32[256,1024]{1,0:T(8,128)S(1)}, u32[]{:S(2)}, u32[]{:S(2)}) collective-permute-start(f32[256,1024]{1,0:T(8,128)S(1)} %slice.127.refs_0_.refs_5_), channel_id=1, source_target_pairs={{0,8},{2,10},{4,12},{6,14},{8,16},{10,18},{12,20},{14,22},{16,24},... | collective-permute-start | bytes 3145736 | tf_op jit(solution)/shard_map/ppermute | solution.py:147
  52.5 26.6 %collective-permute-done = f32[128,3072]{1,0:T(8,128)} collective-permute-done((f32[128,3072]{1,0:T(8,128)}, f32[128,3072]{1,0:T(8,128)}, u32[]{:S(2)}, u32[]{:S(2)}) %collective-permute-start) | collective-permute-done | bytes 1572896 | tf_op jit(solution)/shard_map/ppermute | solution.py:187
  79.1 1.9 pad_maximum_fusion
  82.2 3.8 %collective-permute-start.1 = (f32[256,1024]{1,0:T(8,128)}, f32[256,1024]{1,0:T(8,128)S(1)}, u32[]{:S(2)}, u32[]{:S(2)}) collective-permute-start(f32[256,1024]{1,0:T(8,128)} %slice.124.refs_0_.refs_5_), channel_id=1, source_target_pairs={{0,8},{2,10},{4,12},{6,14},{8,16},{10,18},{12,20},{14,22},{16,24},... | collective-permute-start | bytes 3145736 | tf_op jit(solution)/shard_map/ppermute | solution.py:147
  86.0 2.0 broadcast_select_fusion
  89.5 18.3 %collective-permute-done.1.refs_1_.refs_6_ = f32[256,1024]{1,0:T(8,128)S(1)} collective-permute-done((f32[256,1024]{1,0:T(8,128)}, f32[256,1024]{1,0:T(8,128)S(1)}, u32[]{:S(2)}, u32[]{:S(2)}) %collective-permute-start.1) | collective-permute-done | bytes 1048608 | tf_op jit(solution)/shard_map/ppermute | solution.py:147
  107.8 4.2 %broadcast_select_fusion.1 = (f32[256,1024]{1,0:T(8,128)}, f32[256,1024]{1,0:T(8,128)}, f32[256,1024]{1,0:T(8,128)}, f32[256,1024]{1,0:T(8,128)}) fusion(f32[256,1024]{1,0:T(8,128)S(1)} %collective-permute-done.1.refs_1_.refs_6_, pred[]{:T(512)S(6)} %eq.17, f32[256,3072]{1,0:T(8,128)} %copy-done.7, pred[]{:T(512)S(6)} %eq.18), kind=kLoop, calls=%fused_computation.29 | loop fusion | flops 524288 | bytes 8388610 | tf_op jit(solution)/shard_map/jit(_where)/select_n | solution.py:195
  114.4 21.0 %collective-permute-done.2.refs_2_.refs_7_ = f32[256,1024]{1,0:T(8,128)} collective-permute-done((f32[256,1024]{1,0:T(8,128)}, f32[256,1024]{1,0:T(8,128)}, u32[]{:S(2)}, u32[]{:S(2)}) %collective-permute-start.2) | collective-permute-done | bytes 1048608 | tf_op jit(solution)/shard_map/ppermute | solution.py:147
  137.9 24.5 %shard_map.85 = (f32[256,1024]{1,0:T(8,128)S(1)}, f32[256,1024]{1,0:T(8,128)S(1)}, f32[256,512]{1,0:T(8,128)S(1)}, f32[256,512]{1,0:T(8,128)S(1)}, f32[256,512]{...) custom-call(s32[256,1]{1,0:T(8,128)S(1)} %copy.9.low_ref, ...), custom_call_target="tpu_custom_call" | custom-call | flops 24159191040 | bytes 14680064 | tf_op jit(solution)/shard_map/pallas_call | solution.py:112
  164.1 24.7 %shard_map.84 = (f32[256,1024]{1,0:T(8,128)S(1)}, f32[256,1024]{1,0:T(8,128)S(1)}, f32[256,512]{1,0:T(8,128)S(1)}, f32[256,512]{1,0:T(8,128)S(1)}, f32[256,512]{...) custom-call(s32[256,1]{1,0:T(8,128)S(1)} %copy.9.low_ref, ...), custom_call_target="tpu_custom_call" | custom-call | flops 24159191040 | bytes 14680064 | tf_op jit(solution)/shard_map/pallas_call | solution.py:112
  193.7 22.3 %collective-permute-done.17 = f32[256,1024]{1,0:T(8,128)S(1)} collective-permute-done((f32[256,1024]{1,0:T(8,128)S(1)}, f32[256,1024]{1,0:T(8,128)S(1)}, u32[]{:S(2)}, u32[]{:S(2)}) %collective-permute-start.17) | collective-permute-done | bytes 1048608 | tf_op jit(solution)/shard_map/ppermute | solution.py:147
  217.7 20.5 %collective-permute-done.12 = f32[256,1024]{1,0:T(8,128)S(1)} collective-permute-done((f32[256,1024]{1,0:T(8,128)S(1)}, f32[256,1024]{1,0:T(8,128)S(1)}, u32[]{:S(2)}, u32[]{:S(2)}) %collective-permute-start.12) | collective-permute-done | bytes 1048608 | tf_op jit(solution)/shard_map/ppermute | solution.py:147
  239.7 3.6 %collective-permute-done.18 = f32[256,1024]{1,0:T(8,128)S(1)} collective-permute-done((f32[256,1024]{1,0:T(8,128)S(1)}, f32[256,1024]{1,0:T(8,128)S(1)}, u32[]{:S(2)}, u32[]{:S(2)}) %collective-permute-start.18) | collective-permute-done | bytes 1048608 | tf_op jit(solution)/shard_map/ppermute | solution.py:147
  243.9 1.6 collective-permute-start.19
  245.5 20.3 %collective-permute-done.13 = f32[256,1024]{1,0:T(8,128)S(1)} collective-permute-done((f32[256,1024]{1,0:T(8,128)S(1)}, f32[256,1024]{1,0:T(8,128)S(1)}, u32[]{:S(2)}, u32[]{:S(2)}) %collective-permute-start.13) | collective-permute-done | bytes 1048608 | tf_op jit(solution)/shard_map/ppermute | solution.py:147
  266.4 1.6 collective-permute-start.14
  268.3 13.1 %collective-permute-done.19 = f32[128,3072]{1,0:T(8,128)S(1)} collective-permute-done((f32[128,3072]{1,0:T(8,128)S(1)}, f32[128,3072]{1,0:T(8,128)S(1)}, u32[]{:S(2)}, u32[]{:S(2)}) %collective-permute-start.19) | collective-permute-done | bytes 1572896 | tf_op jit(solution)/shard_map/ppermute | solution.py:213
  281.4 31.3 %collective-permute-done.14 = f32[128,3072]{1,0:T(8,128)S(1)} collective-permute-done((f32[128,3072]{1,0:T(8,128)S(1)}, f32[128,3072]{1,0:T(8,128)S(1)}, u32[]{:S(2)}, u32[]{:S(2)}) %collective-permute-start.14) | collective-permute-done | bytes 1572896 | tf_op jit(solution)/shard_map/ppermute | solution.py:213
  314.5 2.3 maximum_select_fusion
  (92 shorter events, 25.1 us)
Async XLA Ops:
  7.8 38.3 %collective-permute-start.5 = (f32[128,3072]{1,0:T(8,128)S(1)}, f32[128,3072]{1,0:T(8,128)S(1)}, u32[]{:S(2)}, u32[]{:S(2)}) collective-permute-start(f32[128,3072]{1,0:T(8,128)S(1)} %pad_maximum_fusion.7), channel_id=1, source_target_pairs={{0,1},{1,0},{2,3},{3,2},{4,5},{5,4},{6,7},{7,6},{8,9},{9,8},{10,11... | collective-permute-start | bytes 4718600 | tf_op jit(solution)/shard_map/ppermute | solution.py:187
  12.1 67.0 %collective-permute-start = (f32[128,3072]{1,0:T(8,128)}, f32[128,3072]{1,0:T(8,128)}, u32[]{:S(2)}, u32[]{:S(2)}) collective-permute-start(f32[128,3072]{1,0:T(8,128)} %pad_maximum_fusion.6), channel_id=1, source_target_pairs={{0,1},{1,0},{2,3},{3,2},{4,5},{5,4},{6,7},{7,6},{8,9},{9,8},{10,11... | collective-permute-start | bytes 4718600 | tf_op jit(solution)/shard_map/ppermute | solution.py:187
  48.1 31.0 %copy-start.10 = (f32[128,1024]{1,0:T(8,128)S(1)}, f32[128,1024]{1,0:T(8,128)}, u32[]{:S(2)}) copy-start(f32[128,1024]{1,0:T(8,128)} %get-tuple-element.60) | copy-start | bytes 1572868
  48.2 32.8 %copy-start.3 = (f32[256,1024]{1,0:T(8,128)}, f32[256,1024]{1,0:T(8,128)S(1)}, u32[]{:S(2)}) copy-start(f32[256,1024]{1,0:T(8,128)S(1)} %slice.127.refs_0_.refs_5_) | copy-start | bytes 3145732
  48.2 37.8 %collective-permute-start.6 = (f32[256,1024]{1,0:T(8,128)S(1)}, f32[256,1024]{1,0:T(8,128)S(1)}, u32[]{:S(2)}, u32[]{:S(2)}) collective-permute-start(f32[256,1024]{1,0:T(8,128)S(1)} %slice.127.refs_0_.refs_5_), channel_id=1, source_target_pairs={{0,8},{2,10},{4,12},{6,14},{8,16},{10,18},{12,20},{14,22},{16,24},... | collective-permute-start | bytes 3145736 | tf_op jit(solution)/shard_map/ppermute | solution.py:147
  81.0 7.0 %copy-start.7 = (f32[256,3072]{1,0:T(8,128)}, f32[256,3072]{1,0:T(8,128)S(1)}, u32[]{:S(2)}) copy-start(f32[256,3072]{1,0:T(8,128)S(1)} %pad_maximum_fusion) | copy-start | bytes 9437188
  82.2 25.5 %collective-permute-start.1 = (f32[256,1024]{1,0:T(8,128)}, f32[256,1024]{1,0:T(8,128)S(1)}, u32[]{:S(2)}, u32[]{:S(2)}) collective-permute-start(f32[256,1024]{1,0:T(8,128)} %slice.124.refs_0_.refs_5_), channel_id=1, source_target_pairs={{0,8},{2,10},{4,12},{6,14},{8,16},{10,18},{12,20},{14,22},{16,24},... | collective-permute-start | bytes 3145736 | tf_op jit(solution)/shard_map/ppermute | solution.py:147
  88.0 25.5 %collective-permute-start.7 = (f32[256,1024]{1,0:T(8,128)}, f32[256,1024]{1,0:T(8,128)}, u32[]{:S(2)}, u32[]{:S(2)}) collective-permute-start(f32[256,1024]{1,0:T(8,128)} %get-tuple-element.55), channel_id=1, source_target_pairs={{0,4},{2,6},{4,0},{6,2},{8,12},{10,14},{12,8},{14,10},{16,20},{18,... | collective-permute-start | bytes 3145736 | tf_op jit(solution)/shard_map/ppermute | solution.py:147
  89.5 24.0 %copy-start.13 = (s32[256]{0:T(256)S(1)}, s32[256]{0:T(256)}, u32[]{:S(2)}) copy-start(s32[256]{0:T(256)} %param.9) | copy-start | bytes 3076
  89.5 46.0 %collective-permute-start.8 = (f32[256,1024]{1,0:T(8,128)}, f32[256,1024]{1,0:T(8,128)}, u32[]{:S(2)}, u32[]{:S(2)}) collective-permute-start(f32[256,1024]{1,0:T(8,128)} %get-tuple-element.54), channel_id=1, source_target_pairs={{0,2},{2,0},{4,6},{6,4},{8,10},{10,8},{12,14},{14,12},{16,18},{18,... | collective-permute-start | bytes 3145736 | tf_op jit(solution)/shard_map/ppermute | solution.py:147
  112.0 23.4 %collective-permute-start.2 = (f32[256,1024]{1,0:T(8,128)}, f32[256,1024]{1,0:T(8,128)}, u32[]{:S(2)}, u32[]{:S(2)}) collective-permute-start(f32[256,1024]{1,0:T(8,128)} %get-tuple-element.53), channel_id=1, source_target_pairs={{0,4},{2,6},{4,0},{6,2},{8,12},{10,14},{12,8},{14,10},{16,20},{18,... | collective-permute-start | bytes 3145736 | tf_op jit(solution)/shard_map/ppermute | solution.py:147
  113.5 21.9 %collective-permute-start.9 = (f32[256,1024]{1,0:T(8,128)}, f32[256,1024]{1,0:T(8,128)}, u32[]{:S(2)}, u32[]{:S(2)}) collective-permute-start(f32[256,1024]{1,0:T(8,128)} %collective-permute-done.7.refs_2_.refs_7_), channel_id=1, source_target_pairs={{0,2},{2,0},{4,6},{6,4},{8,10},{10,8},{12,14},{14,12},{16,18},{18,... | collective-permute-start | bytes 3145736 | tf_op jit(solution)/shard_map/ppermute | solution.py:147
  113.9 49.2 %collective-permute-start.3 = (f32[256,1024]{1,0:T(8,128)}, f32[256,1024]{1,0:T(8,128)S(1)}, u32[]{:S(2)}, u32[]{:S(2)}) collective-permute-start(f32[256,1024]{1,0:T(8,128)} %get-tuple-element.52), channel_id=1, source_target_pairs={{0,2},{2,0},{4,6},{6,4},{8,10},{10,8},{12,14},{14,12},{16,18},{18,... | collective-permute-start | bytes 3145736 | tf_op jit(solution)/shard_map/ppermute | solution.py:147
  135.4 27.7 %collective-permute-start.4 = (f32[256,1024]{1,0:T(8,128)}, f32[256,1024]{1,0:T(8,128)S(1)}, u32[]{:S(2)}, u32[]{:S(2)}) collective-permute-start(f32[256,1024]{1,0:T(8,128)} %collective-permute-done.2.refs_2_.refs_7_), channel_id=1, source_target_pairs={{0,2},{2,0},{4,6},{6,4},{8,10},{10,8},{12,14},{14,12},{16,18},{18,... | collective-permute-start | bytes 3145736 | tf_op jit(solution)/shard_map/ppermute | solution.py:147
  162.5 27.3 %collective-permute-start.16 = (f32[256,1024]{1,0:T(8,128)S(1)}, f32[256,1024]{1,0:T(8,128)S(1)}, u32[]{:S(2)}, u32[]{:S(2)}) collective-permute-start(f32[256,1024]{1,0:T(8,128)S(1)} %pad_maximum_fusion.11), channel_id=1, source_target_pairs={{0,2},{2,0},{4,6},{6,4},{8,10},{10,8},{12,14},{14,12},{16,18},{18,... | collective-permute-start | bytes 3145736 | tf_op jit(solution)/shard_map/ppermute | solution.py:147
  188.9 3.1 collective-permute-start.11
  189.8 3.9 %collective-permute-start.15 = (f32[256,1024]{1,0:T(8,128)S(1)}, f32[256,1024]{1,0:T(8,128)S(1)}, u32[]{:S(2)}, u32[]{:S(2)}) collective-permute-start(f32[256,1024]{1,0:T(8,128)S(1)} %pad_maximum_fusion.10), channel_id=1, source_target_pairs={{0,2},{2,0},{4,6},{6,4},{8,10},{10,8},{12,14},{14,12},{16,18},{18,... | collective-permute-start | bytes 3145736 | tf_op jit(solution)/shard_map/ppermute | solution.py:147
  190.0 26.0 %collective-permute-start.17 = (f32[256,1024]{1,0:T(8,128)S(1)}, f32[256,1024]{1,0:T(8,128)S(1)}, u32[]{:S(2)}, u32[]{:S(2)}) collective-permute-start(f32[256,1024]{1,0:T(8,128)S(1)} %maximum_add_fusion.4), channel_id=1, source_target_pairs={{0,4},{2,6},{4,0},{6,2},{8,12},{10,14},{12,8},{14,10},{16,20},{18,... | collective-permute-start | bytes 3145736 | tf_op jit(solution)/shard_map/ppermute | solution.py:147
  191.7 26.0 %collective-permute-start.10 = (f32[256,1024]{1,0:T(8,128)S(1)}, f32[256,1024]{1,0:T(8,128)S(1)}, u32[]{:S(2)}, u32[]{:S(2)}) collective-permute-start(f32[256,1024]{1,0:T(8,128)S(1)} %pad_maximum_fusion.8), channel_id=1, source_target_pairs={{0,2},{2,0},{4,6},{6,4},{8,10},{10,8},{12,14},{14,12},{16,18},{18,... | collective-permute-start | bytes 3145736 | tf_op jit(solution)/shard_map/ppermute | solution.py:147
  192.1 46.0 %collective-permute-start.12 = (f32[256,1024]{1,0:T(8,128)S(1)}, f32[256,1024]{1,0:T(8,128)S(1)}, u32[]{:S(2)}, u32[]{:S(2)}) collective-permute-start(f32[256,1024]{1,0:T(8,128)S(1)} %maximum_add_fusion.1), channel_id=1, source_target_pairs={{0,4},{2,6},{4,0},{6,2},{8,12},{10,14},{12,8},{14,10},{16,20},{18,... | collective-permute-start | bytes 3145736 | tf_op jit(solution)/shard_map/ppermute | solution.py:147
  216.3 27.0 %collective-permute-start.18 = (f32[256,1024]{1,0:T(8,128)S(1)}, f32[256,1024]{1,0:T(8,128)S(1)}, u32[]{:S(2)}, u32[]{:S(2)}) collective-permute-start(f32[256,1024]{1,0:T(8,128)S(1)} %fusion.5), channel_id=1, source_target_pairs={{8,0},{10,2},{12,4},{14,6},{16,8},{18,10},{20,12},{22,14},{24,16},... | collective-permute-start | bytes 3145736 | tf_op jit(solution)/shard_map/ppermute | solution.py:147
  238.4 27.4 %collective-permute-start.13 = (f32[256,1024]{1,0:T(8,128)S(1)}, f32[256,1024]{1,0:T(8,128)S(1)}, u32[]{:S(2)}, u32[]{:S(2)}) collective-permute-start(f32[256,1024]{1,0:T(8,128)S(1)} %fusion.2), channel_id=1, source_target_pairs={{8,0},{10,2},{12,4},{14,6},{16,8},{18,10},{20,12},{22,14},{24,16},... | collective-permute-start | bytes 3145736 | tf_op jit(solution)/shard_map/ppermute | solution.py:147
  243.9 37.4 %collective-permute-start.19 = (f32[128,3072]{1,0:T(8,128)S(1)}, f32[128,3072]{1,0:T(8,128)S(1)}, u32[]{:S(2)}, u32[]{:S(2)}) collective-permute-start(f32[128,3072]{1,0:T(8,128)S(1)} %pad_maximum_fusion.2), channel_id=1, source_target_pairs={{0,1},{1,0},{2,3},{3,2},{4,5},{5,4},{6,7},{7,6},{8,9},{9,8},{10,11... | collective-permute-start | bytes 4718600 | tf_op jit(solution)/shard_map/ppermute | solution.py:213
  266.4 46.3 %collective-permute-start.14 = (f32[128,3072]{1,0:T(8,128)S(1)}, f32[128,3072]{1,0:T(8,128)S(1)}, u32[]{:S(2)}, u32[]{:S(2)}) collective-permute-start(f32[128,3072]{1,0:T(8,128)S(1)} %pad_maximum_fusion.4), channel_id=1, source_target_pairs={{0,1},{1,0},{2,3},{3,2},{4,5},{5,4},{6,7},{7,6},{8,9},{9,8},{10,11... | collective-permute-start | bytes 4718600 | tf_op jit(solution)/shard_map/ppermute | solution.py:213
  (11 other events, 23.3 us)
where the time goes:
time: 317 us
  waiting for transfers between devices  211 us (67%)
  Pallas kernels  49.2 us (16%)
  starting transfers between devices  25.2 us (8%)
  other arithmetic  16.1 us (5%)
  local copies, waits for them, and re-layouts  14.2 us (4%)
    ppermute x16, waiting for transfers between devices, shift_seq(): lax.ppermute(x, 'seq', [(a, b) for a, b in route if 0 <= b < seq_size])  106 us
    ppermute x2, waiting for transfers between devices, per_device(): lax.ppermute(pack(1 - t), 'tp', swap)  60.6 us
    pallas_call x2, Pallas kernels, run_attend(): pl.pallas_call(functools.partial(attend, reach1, group), grid=(heads,), i...  49.2 us
    ppermute x2, waiting for transfers between devices, per_device(): results.append((full[:rows], lax.ppermute(full[rows:], 'tp', swap)))  44.4 us
    ppermute x16, starting transfers between devices, shift_seq(): lax.ppermute(x, 'seq', [(a, b) for a, b in route if 0 <= b < seq_size])  18.9 us
    unnamed x30, local copies, waits for them, and re-layouts  6.81 us
  transfers between devices with their start and end apart: 20, of which 10 were waited for; matrix products, arithmetic and copies ran while one was open for 4% of the time, Pallas kernels for 16%

commit v1 on v0

--- a/solution.py
+++ b/solution.py
@@ -9,7 +9,8 @@
 
 HEAD_DIM = 128
 WINDOW = 1024
-CHUNKS = 2
+LEAD = 5
+MESH = pl.DeviceIdType.MESH
 
 score_scale = 168.0 ** (-0.5)
 neg_fill = -1e30
@@ -131,6 +132,264 @@
     return outs[0], outs[1], outs[2 : 2 + reach1], outs[2 + reach1 :]
 
 
+def fused(heads, group, n, low_ref, pos_ref, kidx_ref, q_hbm, k_hbm, v_hbm, g_hbm, o_hbm, dq_hbm, dk_hbm, dv_hbm,
+          qb, gb, kv, dkv, ob, dqb, r34, rx, rd, s_ref, ph_ref, pl_ref,
+          in_send, in_recv, in_local, up_send, up_recv, cross_send, cross_recv, core_send, core_recv,
+          b34_send, b34_recv, bx_send, bx_recv, bd_send, bd_recv, out_send, out_recv, out_local):
+    d = HEAD_DIM
+    gd = group * d
+    s, t = lax.axis_index("seq"), lax.axis_index("tp")
+    rows = q_hbm.shape[0]
+    c1 = lax.rem(s, 2)
+    x1 = lax.rem(s // 2, 2)
+    mate = {"tp": 1 - t}
+    core = {"seq": s + 1 - 2 * c1}
+    cross = {"seq": s + 2 - 4 * x1}
+    above = {"seq": lax.rem(s + 4, n)}
+    below = {"seq": lax.rem(s + n - 4, n)}
+    has_below, has_above = s >= 4, s < n - 4
+
+    barrier = pltpu.get_barrier_semaphore()
+
+    def greet(who):
+        pl.semaphore_signal(barrier, inc=1, device_id=who, device_id_type=MESH)
+
+    for who in (mate, core, cross, above, below):
+        greet(who)
+    pl.semaphore_wait(barrier, 5)
+
+    def remote(a, b, ss, rs, who):
+        return pltpu.make_async_remote_copy(
+            src_ref=a, dst_ref=b, send_sem=ss, recv_sem=rs, device_id=who, device_id_type=MESH
+        )
+
+    def cols(ref, who, h, width):
+        start = pl.multiple_of(who * (heads * width) + h * width, width)
+        return ref.at[:, pl.ds(start, width)]
+
+    def landing(i, h, half):
+        r = pl.ds(half * rows, rows)
+        if i == 0:
+            return kv.at[h, 0, 0, r, :]
+        if i == 1:
+            return kv.at[h, 0, 1, r, :]
+        return (qb if i == 2 else gb).at[h, r, :]
+
+    in_src = ((k_hbm, d), (v_hbm, d), (q_hbm, gd), (g_hbm, gd))
+
+    def y_in(i, h):
+        ref, w = in_src[i]
+        return remote(cols(ref, 1 - t, h, w), landing(i, h, 1), in_send.at[i, h], in_recv.at[i, h], mate)
+
+    def l_in(i, h):
+        ref, w = in_src[i]
+        return pltpu.make_async_copy(cols(ref, t, h, w), landing(i, h, 0), in_local.at[i, h])
+
+    def up(h):
+        return remote(kv.at[h, 0], kv.at[h, 1], up_send.at[h], up_recv.at[h], above)
+
+    def over(h):
+        return remote(kv.at[h, x1], kv.at[h, 2], cross_send.at[h], cross_recv.at[h], cross)
+
+    def near(i, h):
+        a = kv.at[h, c1] if i == 0 else kv.at[h, 2]
+        return remote(a, kv.at[h, 3 + i], core_send.at[i, h], core_recv.at[i, h], core)
+
+    def b34(h):
+        return remote(dkv.at[h, pl.ds(3, 2)], r34.at[h], b34_send.at[h], b34_recv.at[h], core)
+
+    def bx(h):
+        return remote(dkv.at[h, 2], rx.at[h], bx_send.at[h], bx_recv.at[h], cross)
+
+    def bd(h):
+        return remote(dkv.at[h, 1], rd.at[h], bd_send.at[h], bd_recv.at[h], below)
+
+    out_dst = ((o_hbm, gd), (dq_hbm, gd), (dk_hbm, d), (dv_hbm, d))
+
+    def leaving(i, h, half):
+        r = pl.ds(half * rows, rows)
+        if i < 2:
+            return (ob if i == 0 else dqb).at[h, r, :]
+        return dkv.at[h, 0, i - 2, r, :]
+
+    def y_out(i, h):
+        ref, w = out_dst[i]
+        return remote(leaving(i, h, 1), cols(ref, t, h, w), out_send.at[i, h], out_recv.at[i, h], mate)
+
+    def l_out(i, h):
+        ref, w = out_dst[i]
+        return pltpu.make_async_copy(leaving(i, h, 0), cols(ref, t, h, w), out_local.at[i, h])
+
+    def each(body):
+        def run(h, carry):
+            body(h)
+            return carry
+
+        lax.fori_loop(0, heads, run, 0)
+
+    def begin(kinds):
+        def body(h):
+            for i in kinds:
+                y_in(i, h).start()
+                l_in(i, h).start()
+
+        each(body)
+
+    begin((0, 1))
+    begin((2, 3))
+
+    def stage_a(h):
+        for i in (0, 1):
+            l_in(i, h).wait()
+            y_in(i, h).wait_recv()
+
+        @pl.when(has_above)
+        def _():
+            up(h).start()
+
+    def stage_b(h):
+        @pl.when(has_below)
+        def _():
+            up(h).wait_recv()
+
+        @pl.when(jnp.logical_not(has_below))
+        def _():
+            kv[h, 1] = jnp.zeros(kv.shape[2:], f32)
+
+        over(h).start()
+        near(0, h).start()
+
+    def stage_c(h):
+        over(h).wait_recv()
+        near(1, h).start()
+
+    def compute(h):
+        for i in (2, 3):
+            l_in(i, h).wait()
+            y_in(i, h).wait_recv()
+        for i in (0, 1):
+            near(i, h).wait_recv()
+        attend(
+            5, group, low_ref, pos_ref, kidx_ref, qb.at[h], gb.at[h],
+            *[kv.at[h, j, 0] for j in range(5)],
+            *[kv.at[h, j, 1] for j in range(5)],
+            ob.at[h], dqb.at[h],
+            *[dkv.at[h, j, 0] for j in range(5)],
+            *[dkv.at[h, j, 1] for j in range(5)],
+            s_ref, ph_ref, pl_ref,
+        )
+        b34(h).start()
+        for i in (0, 1):
+            y_out(i, h).start()
+            l_out(i, h).start()
+
+    def stage_e2(h):
+        b34(h).wait()
+        dkv[h, 2] = dkv[h, 2] + r34[h, 1]
+        dkv[h, c1] = dkv[h, c1] + r34[h, 0]
+        bx(h).start()
+
+    def stage_e3(h):
+        bx(h).wait()
+        dkv[h, x1] = dkv[h, x1] + rx[h]
+
+        @pl.when(has_below)
+        def _():
+            bd(h).start()
+
+    def stage_e4(h):
+        @pl.when(has_above)
+        def _():
+            bd(h).wait_recv()
+            dkv[h, 0] = dkv[h, 0] + rd[h]
+
+        for i in (2, 3):
+            y_out(i, h).start()
+            l_out(i, h).start()
+
+    stages = STAGES(stage_a, stage_b, stage_c, compute, stage_e2, stage_e3, stage_e4)
+    last = max(lag for lag, _ in stages)
+
+    def step(i, carry):
+        for lag, stage in stages:
+            @pl.when((i >= lag) & (i < lag + heads))
+            def _():
+                stage(i - lag)
+
+        return carry
+
+    lax.fori_loop(0, heads + last, step, 0)
+
+    def finish(h):
+        for i in range(4):
+            y_in(i, h).wait_send()
+            y_out(i, h).wait()
+            l_out(i, h).wait()
+        over(h).wait_send()
+        near(0, h).wait_send()
+        near(1, h).wait_send()
+
+        @pl.when(has_above)
+        def _():
+            up(h).wait_send()
+
+        @pl.when(has_below)
+        def _():
+            bd(h).wait_send()
+
+    each(finish)
+
+
+def STAGES(a, b, c, compute, e2, e3, e4):
+    return ((0, a), (1, b), (2, c), (LEAD, compute), (LEAD + 1, e2), (LEAD + 2, e3), (LEAD + 3, e4))
+
+
+def run_fused(low, pos, kidx, queries, keys, values, out_grad):
+    rows = queries.shape[0]
+    tok = 2 * rows
+    d = HEAD_DIM
+    heads = keys.shape[1] // (2 * d)
+    group = queries.shape[1] // keys.shape[1]
+    gd = group * d
+    n = lax.axis_size("seq")
+    vm = pl.BlockSpec(memory_space=pltpu.VMEM)
+    hbm = pl.BlockSpec(memory_space=pl.ANY)
+    dma = lambda *shape: pltpu.SemaphoreType.DMA(shape)
+    flops = 2 * 6 * 3 * tok * group * tok * 5 * d * heads
+    return pl.pallas_call(
+        functools.partial(fused, heads, group, n),
+        in_specs=[vm] * 3 + [hbm] * 4,
+        out_specs=[hbm] * 4,
+        out_shape=[jax.ShapeDtypeStruct(x.shape, f32) for x in (queries, queries, keys, values)],
+        scratch_shapes=[
+            pltpu.VMEM((heads, tok, gd), f32),
+            pltpu.VMEM((heads, tok, gd), f32),
+            pltpu.VMEM((heads, 5, 2, tok, d), f32),
+            pltpu.VMEM((heads, 5, 2, tok, d), f32),
+            pltpu.VMEM((heads, tok, gd), f32),
+            pltpu.VMEM((heads, tok, gd), f32),
+            pltpu.VMEM((heads, 2, 2, tok, d), f32),
+            pltpu.VMEM((heads, 2, tok, d), f32),
+            pltpu.VMEM((heads, 2, tok, d), f32),
+            pltpu.VMEM((5, group * tok, tok), f32),
+            pltpu.VMEM((5, group * tok, tok), bf16),
+            pltpu.VMEM((5, group * tok, tok), bf16),
+            dma(4, heads), dma(4, heads), dma(4, heads),
+            dma(heads), dma(heads),
+            dma(heads), dma(heads),
+            dma(2, heads), dma(2, heads),
+            dma(heads), dma(heads),
+            dma(heads), dma(heads),
+            dma(heads), dma(heads),
+            dma(4, heads), dma(4, heads), dma(4, heads),
+        ],
+        compiler_params=pltpu.CompilerParams(
+            vmem_limit_bytes=58 * 2**20, collective_id=0, has_side_effects=True
+        ),
+        cost_estimate=pl.CostEstimate(flops=flops, bytes_accessed=48 * queries.size, transcendentals=0),
+    )(low, pos, kidx, queries, keys, values, out_grad)
+
+
 def per_device(queries, keys, values, out_grad, positions):
     seq_size, tp_size = lax.axis_size("seq"), lax.axis_size("tp")
     s = lax.axis_index("seq")
@@ -138,10 +397,7 @@
     rows = queries.shape[0]
     tok = rows * tp_size
     pair = tp_size == 2
-    kv_local = keys.shape[1] // tp_size
-    q_local = queries.shape[1] // tp_size
-    chunks = CHUNKS if pair else 1
-    kw, qw = kv_local // chunks, q_local // chunks
+    kw = keys.shape[1] // tp_size
 
     def shift_seq(x, route):
         return lax.ppermute(x, "seq", [(a, b) for a, b in route if 0 <= b < seq_size])
@@ -150,7 +406,6 @@
     down = [(i, i - 4) for i in range(seq_size)]
     cross = [(i, i ^ 2) for i in range(seq_size)]
     core = [(i, i ^ 1) for i in range(seq_size)]
-    swap = [(0, 1), (1, 0)]
 
     local = jnp.arange(tok, dtype=jnp.int32)
     if pair:
@@ -164,72 +419,39 @@
     b = s % 4
     base = s - b
     x1, c1 = b // 2 == 1, b % 2 == 1
-    p2_block = jnp.where(x1, s - 2, s - 2)
+    p2_block = s - 2
     c_p2 = (s ^ 1) - 2
     c_first = jnp.where(c1, s - 1, s - 3)
     blocks = jnp.stack([s, s - 4, p2_block, c_first, c_p2])
     kidx = blocks[:, None] * tok + local[None, :]
 
     pos, low = pos[:, None], low[:, None]
-
-    results = []
-    for c in range(chunks):
-        if pair:
-            def part(x, width, who):
-                return lax.dynamic_slice_in_dim(x, who * width * chunks + c * width, width, 1)
-
-            def pack(who):
-                return jnp.concatenate(
-                    [part(queries, qw, who), part(out_grad, qw, who), part(keys, kw, who), part(values, kw, who)],
-                    axis=1,
-                )
-
-            packed = jnp.concatenate([pack(t), lax.ppermute(pack(1 - t), "tp", swap)], axis=0)
-            q, grad, own = packed[:, :qw], packed[:, qw : 2 * qw], packed[:, 2 * qw :]
-        else:
-            a2a = lambda x: lax.all_to_all(x, "tp", split_axis=1, concat_axis=0, tiled=True)
-            q, grad = a2a(queries), a2a(out_grad)
-            own = jnp.concatenate([a2a(keys), a2a(values)], axis=1)
-        prior = shift_seq(own, up)
-        crossed = shift_seq(jnp.where(x1, prior, own), cross)
-        near = shift_seq(jnp.where(c1, prior, own), core)
-        near_crossed = shift_seq(crossed, core)
-        pieces = [own, prior, crossed, near, near_crossed]
-        out, dq, dks, dvs = run_attend(low, pos, kidx, q, grad, pieces)
-        g_own, g_prior, g_crossed, g_near, g_nc = [
-            jnp.concatenate([dk, dv], axis=1) for dk, dv in zip(dks, dvs)
-        ]
-        near_back = shift_seq(g_near, core)
-        g_crossed = g_crossed + shift_seq(g_nc, core)
-        zero = jnp.zeros_like(g_own)
-        g_own = g_own + jnp.where(c1, zero, near_back)
-        g_prior = g_prior + jnp.where(c1, near_back, zero)
-        cross_back = shift_seq(g_crossed, cross)
-        g_own = g_own + jnp.where(x1, zero, cross_back)
-        g_prior = g_prior + jnp.where(x1, cross_back, zero)
-        g_own = g_own + shift_seq(g_prior, down)
-        if pair:
-            full = jnp.concatenate([out, dq, g_own], axis=1)
-            results.append((full[:rows], lax.ppermute(full[rows:], "tp", swap)))
-        else:
-            b2a = lambda x: lax.all_to_all(x, "tp", split_axis=0, concat_axis=1, tiled=True)
-            return (b2a(out), b2a(dq), b2a(g_own[:, :kw]), b2a(g_own[:, kw:]))
-
-    def gather(begin, width):
-        mine = jnp.concatenate([r[0][:, begin : begin + width] for r in results], axis=1)
-        theirs = jnp.concatenate([r[1][:, begin : begin + width] for r in results], axis=1)
-        return jnp.where(
-            t == 0,
-            jnp.concatenate([mine, theirs], axis=1),
-            jnp.concatenate([theirs, mine], axis=1),
-        )
-
-    return (
-        gather(0, qw),
-        gather(qw, qw),
-        gather(2 * qw, kw),
-        gather(2 * qw + kw, kw),
-    )
+    if pair:
+        return tuple(run_fused(low, pos, kidx, queries, keys, values, out_grad))
+
+    a2a = lambda x: lax.all_to_all(x, "tp", split_axis=1, concat_axis=0, tiled=True)
+    b2a = lambda x: lax.all_to_all(x, "tp", split_axis=0, concat_axis=1, tiled=True)
+    q, grad = a2a(queries), a2a(out_grad)
+    own = jnp.concatenate([a2a(keys), a2a(values)], axis=1)
+    prior = shift_seq(own, up)
+    crossed = shift_seq(jnp.where(x1, prior, own), cross)
+    near = shift_seq(jnp.where(c1, prior, own), core)
+    near_crossed = shift_seq(crossed, core)
+    pieces = [own, prior, crossed, near, near_crossed]
+    out, dq, dks, dvs = run_attend(low, pos, kidx, q, grad, pieces)
+    g_own, g_prior, g_crossed, g_near, g_nc = [
+        jnp.concatenate([dk, dv], axis=1) for dk, dv in zip(dks, dvs)
+    ]
+    near_back = shift_seq(g_near, core)
+    g_crossed = g_crossed + shift_seq(g_nc, core)
+    zero = jnp.zeros_like(g_own)
+    g_own = g_own + jnp.where(c1, zero, near_back)
+    g_prior = g_prior + jnp.where(c1, near_back, zero)
+    cross_back = shift_seq(g_crossed, cross)
+    g_own = g_own + jnp.where(x1, zero, cross_back)
+    g_prior = g_prior + jnp.where(x1, cross_back, zero)
+    g_own = g_own + shift_seq(g_prior, down)
+    return (b2a(out), b2a(dq), b2a(g_own[:, :kw]), b2a(g_own[:, kw:]))
 
 
 def solution(mesh):

time: 317 us -> 158 us (0.50)
  waiting for transfers between devices: 211 us -> 0 us
  Pallas kernels: 49.2 us -> 145 us
  starting transfers between devices: 25.2 us -> 0 us
  other arithmetic: 16.1 us -> 2.06 us
  local copies, waits for them, and re-layouts: 14.2 us -> 9.44 us
    ppermute x20 -> x0, waiting for transfers between devices: 211 us -> none  [the longest x16 106 us: shift_seq(): lax.ppermute(x, 'seq', [(a, b) for a, b in route if 0 <= b < seq_size])]
    pallas_call x2 -> x1, Pallas kernels: 49.2 us -> 145 us  [run_fused(): pl.pallas_call(functools.partial(fused, heads, group, n), in_specs=[vm] *...]
    ppermute x20 -> x0, starting transfers between devices: 25.2 us -> none  [the longest x16 18.9 us: shift_seq(): lax.ppermute(x, 'seq', [(a, b) for a, b in route if 0 <= b < seq_size])]
    select_n x4 -> x0, other arithmetic: 10.1 us -> none  [the longest x2 6.2 us: per_device(): near = shift_seq(jnp.where(c1, prior, own), core)]
    dynamic_slice x4 -> x0, local copies, waits for them, and re-layouts: 5.34 us -> none  [part(): lax.dynamic_slice_in_dim(x, who * width * chunks + c * width, width, 1)]
    concatenate x10 -> x0, other arithmetic: 4.1 us -> none  [the longest x2 2.19 us: per_device(): jnp.concatenate([pack(t), lax.ppermute(pack(1 - t), 'tp', swap)], axis=0)]
    unnamed x30 -> x10, local copies, waits for them, and re-layouts: 6.81 us -> 7.79 us
  transfers between devices with their start and end apart: 20 -> 0, of which waited for: 10 -> 0; matrix products, arithmetic and copies ran while one was open for 4% -> 0% of each run, Pallas kernels for 16% -> 0%
where the time goes in v1:
time: 158 us; the launch traced here: 157 us
  Pallas kernels  145 us (92%)
  local copies, waits for them, and re-layouts  9.44 us (6%)
  other arithmetic  2.06 us (1%)
    pallas_call x1, Pallas kernels, run_fused(): pl.pallas_call(functools.partial(fused, heads, group, n), in_specs=[vm] *...  145 us
    unnamed x10, local copies, waits for them, and re-layouts  7.79 us

profile of v1, /device:TPU:0, one launch (start us, length us, event | category | flops | bytes accessed | tf_op | source)
XLA Modules:
  0.0 157.3 jit_solution(7359630140332329284)
XLA Ops:
  0.7 0.1 stack.23
  0.8 0.8 fusion.6
  1.5 0.7 compare_select_fusion
  2.2 0.7 broadcast_add_fusion.kidx_ref
  2.9 0.8 copy.9.low_ref
  3.7 0.7 fusion.1.pos_ref
  4.4 145.1 %shard_map.84 = (f32[128,4096]{1,0:T(8,128)}, f32[128,4096]{1,0:T(8,128)}, f32[128,2048]{1,0:T(8,128)}, f32[128,2048]{1,0:T(8,128)}) custom-call(s32[256,1]{1,0:T(8,128)} %copy.9.low_ref, s32[256,1]{1,0:T(8,128)} %fusion.1.pos_ref, s32[5,256]{1,0:T(8,128)} %broadcast_add_fusion.kidx_ref, f32[128,4096]{1,0:T(8,128)} %q_hbm.1, f32[128,2048]{1,0:T(8,128)} %k_hbm.1, ...), custom_call_target="tpu_custom_call" | custom-call | flops 24159191040 | bytes 25165824 | tf_op jit(solution)/shard_map/pallas_call | solution.py:359
  149.5 0.0 copy-start
  149.5 3.3 %copy.14 = f32[128,4096]{1,0:T(8,128)} copy(f32[128,4096]{1,0:T(8,128)} %get-tuple-element.12) | data formatting | bytes 4194304
  152.8 0.0 copy-done
  152.8 0.0 copy-start.2
  152.8 1.3 copy.15
  154.1 0.6 copy-done.2
  154.8 0.0 copy-start.1
  154.8 1.0 copy.16
  155.7 0.6 copy-done.1
  156.4 1.0 copy.17
  (1 shorter events, 0.0 us)
Async XLA Ops:
  149.5 3.3 %copy-start = (f32[128,4096]{1,0:T(8,128)S(1)}, f32[128,4096]{1,0:T(8,128)}, u32[]{:S(2)}) copy-start(f32[128,4096]{1,0:T(8,128)} %get-tuple-element.13) | copy-start | bytes 6291460
  152.8 2.0 %copy-start.2 = (f32[128,2048]{1,0:T(8,128)S(1)}, f32[128,2048]{1,0:T(8,128)}, u32[]{:S(2)}) copy-start(f32[128,2048]{1,0:T(8,128)} %get-tuple-element.14) | copy-start | bytes 3145732
  154.8 1.6 %copy-start.1 = (f32[128,2048]{1,0:T(8,128)S(1)}, f32[128,2048]{1,0:T(8,128)}, u32[]{:S(2)}) copy-start(f32[128,2048]{1,0:T(8,128)} %get-tuple-element.15) | copy-start | bytes 3145732

commit v2 on v1

--- a/solution.py
+++ b/solution.py
@@ -132,8 +132,8 @@
     return outs[0], outs[1], outs[2 : 2 + reach1], outs[2 + reach1 :]
 
 
-def fused(heads, group, n, low_ref, pos_ref, kidx_ref, q_hbm, k_hbm, v_hbm, g_hbm, o_hbm, dq_hbm, dk_hbm, dv_hbm,
-          qb, gb, kv, dkv, ob, dqb, r34, rx, rd, s_ref, ph_ref, pl_ref,
+def fused(heads, group, n, positions_ref, q_hbm, k_hbm, v_hbm, g_hbm, o_hbm, dq_hbm, dk_hbm, dv_hbm,
+          qb, gb, kv, dkv, ob, dqb, r34, rx, rd, s_ref, ph_ref, pl_ref, low_ref, pos_ref, kidx_ref,
           in_send, in_recv, in_local, up_send, up_recv, cross_send, cross_recv, core_send, core_recv,
           b34_send, b34_recv, bx_send, bx_recv, bd_send, bd_recv, out_send, out_recv, out_local):
     d = HEAD_DIM
@@ -237,6 +237,21 @@
 
     begin((0, 1))
     begin((2, 3))
+
+    tok = 2 * rows
+
+    def order(axis, shape):
+        i = lax.broadcasted_iota(jnp.int32, shape, axis)
+        return lax.rem(i + t * rows, tok)
+
+    half = lambda who: positions_ref[pl.ds(pl.multiple_of(who * rows, rows), rows), :]
+    since = jnp.concatenate([half(t), half(1 - t)], axis=0)
+    pos = s * tok + order(0, (tok, 1))
+    pos_ref[...] = pos
+    low_ref[...] = jnp.maximum(jnp.maximum(pos - since, pos - (WINDOW - 1)), 0)
+    blocks = (s, s - 4, s - 2, s - 3 + 2 * c1, s - 1 - 2 * c1)
+    for j in range(5):
+        kidx_ref[j : j + 1, :] = blocks[j] * tok + order(1, (1, tok))
 
     def stage_a(h):
         for i in (0, 1):
@@ -344,7 +359,7 @@
     return ((0, a), (1, b), (2, c), (LEAD, compute), (LEAD + 1, e2), (LEAD + 2, e3), (LEAD + 3, e4))
 
 
-def run_fused(low, pos, kidx, queries, keys, values, out_grad):
+def run_fused(positions, queries, keys, values, out_grad):
     rows = queries.shape[0]
     tok = 2 * rows
     d = HEAD_DIM
@@ -358,7 +373,7 @@
     flops = 2 * 6 * 3 * tok * group * tok * 5 * d * heads
     return pl.pallas_call(
         functools.partial(fused, heads, group, n),
-        in_specs=[vm] * 3 + [hbm] * 4,
+        in_specs=[vm] + [hbm] * 4,
         out_specs=[hbm] * 4,
         out_shape=[jax.ShapeDtypeStruct(x.shape, f32) for x in (queries, queries, keys, values)],
         scratch_shapes=[
@@ -374,6 +389,9 @@
             pltpu.VMEM((5, group * tok, tok), f32),
             pltpu.VMEM((5, group * tok, tok), bf16),
             pltpu.VMEM((5, group * tok, tok), bf16),
+            pltpu.VMEM((tok, 1), jnp.int32),
+            pltpu.VMEM((tok, 1), jnp.int32),
+            pltpu.VMEM((5, tok), jnp.int32),
             dma(4, heads), dma(4, heads), dma(4, heads),
             dma(heads), dma(heads),
             dma(heads), dma(heads),
@@ -387,7 +405,7 @@
             vmem_limit_bytes=58 * 2**20, collective_id=0, has_side_effects=True
         ),
         cost_estimate=pl.CostEstimate(flops=flops, bytes_accessed=48 * queries.size, transcendentals=0),
-    )(low, pos, kidx, queries, keys, values, out_grad)
+    )(positions[:, None], queries, keys, values, out_grad)
 
 
 def per_device(queries, keys, values, out_grad, positions):
@@ -396,7 +414,8 @@
     t = lax.axis_index("tp")
     rows = queries.shape[0]
     tok = rows * tp_size
-    pair = tp_size == 2
+    if tp_size == 2:
+        return tuple(run_fused(positions, queries, keys, values, out_grad))
     kw = keys.shape[1] // tp_size
 
     def shift_seq(x, route):
@@ -408,10 +427,6 @@
     core = [(i, i ^ 1) for i in range(seq_size)]
 
     local = jnp.arange(tok, dtype=jnp.int32)
-    if pair:
-        local = lax.rem(local + t * rows, tok)
-        mine, other = positions[:rows], positions[rows:]
-        positions = jnp.where(t == 0, positions, jnp.concatenate([other, mine]))
     first = s * tok
     pos = first + local
     low = jnp.maximum(jnp.maximum(pos - positions, pos - (WINDOW - 1)), 0)
@@ -426,8 +441,6 @@
     kidx = blocks[:, None] * tok + local[None, :]
 
     pos, low = pos[:, None], low[:, None]
-    if pair:
-        return tuple(run_fused(low, pos, kidx, queries, keys, values, out_grad))
 
     a2a = lambda x: lax.all_to_all(x, "tp", split_axis=1, concat_axis=0, tiled=True)
     b2a = lambda x: lax.all_to_all(x, "tp", split_axis=0, concat_axis=1, tiled=True)

time: 158 us -> 156 us (0.987)
  other arithmetic: 2.06 us -> 0 us
where the time goes in v2:
time: 156 us
  Pallas kernels  146 us (94%)
  local copies, waits for them, and re-layouts  9.27 us (6%)
    pallas_call x1, Pallas kernels, run_fused(): pl.pallas_call(functools.partial(fused, heads, group, n), in_specs=[vm] +...  146 us
    unnamed x10, local copies, waits for them, and re-layouts  7.79 us

profile of v2, /device:TPU:0, one launch (start us, length us, event | category | flops | bytes accessed | tf_op | source)
XLA Modules:
  0.0 155.7 jit_solution(17090652883292052130)
XLA Ops:
  0.6 1.5 copy.9.positions_ref
  2.1 145.7 %shard_map.84 = (f32[128,4096]{1,0:T(8,128)}, f32[128,4096]{1,0:T(8,128)}, f32[128,2048]{1,0:T(8,128)}, f32[128,2048]{1,0:T(8,128)}) custom-call(s32[256,1]{1,0:T(8,128)} %copy.9.positions_ref, f32[128,4096]{1,0:T(8,128)} %q_hbm.1, f32[128,2048]{1,0:T(8,128)} %k_hbm.1, f32[128,2048]{1,0:T(8,128)} %v_hbm.1, f32[128,4096]{1,0:T(8,128)} %g_hbm.1), custom_call_target="tpu_custom_call" | custom-call | flops 24159191040 | bytes 25165824 | tf_op jit(solution)/shard_map/pallas_call | solution.py:374
  147.9 0.0 copy-start
  147.9 3.3 %copy.14 = f32[128,4096]{1,0:T(8,128)} copy(f32[128,4096]{1,0:T(8,128)} %get-tuple-element.8) | data formatting | bytes 4194304
  151.1 0.0 copy-done
  151.1 0.0 copy-start.2
  151.1 1.3 copy.15
  152.4 0.6 copy-done.2
  153.1 0.0 copy-start.1
  153.1 1.0 copy.16
  154.1 0.6 copy-done.1
  154.7 1.0 copy.17
Async XLA Ops:
  147.9 3.3 %copy-start = (f32[128,4096]{1,0:T(8,128)S(1)}, f32[128,4096]{1,0:T(8,128)}, u32[]{:S(2)}) copy-start(f32[128,4096]{1,0:T(8,128)} %get-tuple-element.9) | copy-start | bytes 6291460
  151.1 2.0 %copy-start.2 = (f32[128,2048]{1,0:T(8,128)S(1)}, f32[128,2048]{1,0:T(8,128)}, u32[]{:S(2)}) copy-start(f32[128,2048]{1,0:T(8,128)} %get-tuple-element.10) | copy-start | bytes 3145732
  153.1 1.6 %copy-start.1 = (f32[128,2048]{1,0:T(8,128)S(1)}, f32[128,2048]{1,0:T(8,128)}, u32[]{:S(2)}) copy-start(f32[128,2048]{1,0:T(8,128)} %get-tuple-element.11) | copy-start | bytes 3145732
